TPU v7x, 128 devices: a whole 4x4x4 slice. The times are simulated.
128 devices in a mesh: head: 4 (over y_hi, core), blk: 32 (over z, y_lo, x).
Axes of the slice: x: 4, y: 4 (y_hi: 2, y_lo: 2; y = y_hi * 2 + y_lo), z: 4, core: 2. Of those that a mesh axis runs over, the one named last changes fastest.
Arguments:
- queries: bfloat16 [32768, 1536], P(('blk', 'head')), may hold values from -24 to 24
- key_rows: bfloat16 [32768, 1536], P(('blk', 'head')), may hold values from -6 to 6
- value_rows: bfloat16 [32768, 1536], P(('blk', 'head')), may hold values from -6 to 6
- tile_lists: int32 [256, 16], P('blk'), may hold values from 0 to 255, as said below
Outputs:
- attended: bfloat16 [32768, 1536], P(('blk', 'head'))
Inputs may be any that keep to these rules, and one draw needn't show every extreme that they name: `tile_lists`: tile index (f * 2 + i) * 2 + j is frame tile f, height tile i, width tile j. Row t holds 16 distinct tiles whose frame tile lies within 4 of that of tile t, distances counted cyclically over the clip's frame tiles, and t itself among them.
All inputs are finite; a program needn't handle non-finite values.
Results may differ from a plain program's by a relative error of at most 0.0085.
Values may be sent and summed in bfloat16 or wider, within the bound.
A program may use at most 128 MiB of HBM per device.

v0:
```python
import functools

import jax
import jax.numpy as jnp
from jax import lax
from jax.experimental import pallas as pl
from jax.experimental.pallas import tpu as pltpu
from jax.sharding import PartitionSpec as P

MESH = pl.DeviceIdType.MESH
HD = 128
TILE = 128
SEL = 16
GROUP = 3 * HD
ROW = 32
HALO = ROW // 2
EXP2 = HD ** -0.5 * 1.4426950408889634


def kernel(q_hbm, k_hbm, v_hbm, lists_hbm, out_hbm, relay_k, relay_v, relay_q, relay_o, win_k, win_v, win_q, win_o,
           lists_r, lists_v, lists_s, xs, xr, ys, yr, fs, fr, ls, lxr, lyr, lc, oys, oyr, oxs, oxr):
    head, blk = lax.axis_index("head"), lax.axis_index("blk")
    x, y_lo, z = blk % 4, (blk // 4) % 2, blk // 8
    core = head % 2
    y = (head // 2) * 2 + y_lo
    mine = (y + 7 - x) % 4
    active = mine < 3
    own_row = core == y_lo

    def device(dx, dy, dz, dc):
        return {"head": (dy // 2) * 2 + dc, "blk": dz * 8 + (dy % 2) * 4 + dx}

    def remote(src, dst, send, recv, to):
        return pltpu.make_async_remote_copy(
            src_ref=src, dst_ref=dst, send_sem=send, recv_sem=recv, device_id=to, device_id_type=MESH
        )

    def wait(ref, sem):
        pltpu.make_async_copy(ref, ref, sem).wait()

    def either(local, src, dst, send, recv, to):
        @pl.when(local)
        def _():
            pltpu.make_async_copy(src, dst, recv).start()

        @pl.when(jnp.logical_not(local))
        def _():
            remote(src, dst, send, recv, to).start()

    barrier = pltpu.get_barrier_semaphore()
    for d in range(1, 4):
        pl.semaphore_signal(barrier, inc=1, device_id=device((x + d) % 4, y, z, core), device_id_type=MESH)
        for c in range(2):
            pl.semaphore_signal(barrier, inc=1, device_id=device(x, (y + d) % 4, z, c), device_id_type=MESH)
    pl.semaphore_signal(barrier, inc=1, device_id=device(x, y, z, 1 - core), device_id_type=MESH)
    across = device(x, y, (z + 2 * core + 3) % 4, 1 - core)
    pl.semaphore_signal(barrier, inc=1, device_id=across, device_id_type=MESH)
    pl.semaphore_wait(barrier, 11)

    arrays = ((k_hbm, relay_k, win_k, HALO), (v_hbm, relay_v, win_v, HALO), (q_hbm, relay_q, win_q, 0))

    def along_x(a):
        src, relay = arrays[a][:2]
        for d in (2, 1, 3):
            to = (x + d) % 4
            columns = pl.ds(pl.multiple_of(to * GROUP, GROUP), GROUP)
            remote(src.at[:, :, columns], relay.at[x], xs.at[a], xr.at[a, d], device(to, y, z, core)).start()

    def along_y(a, d):
        src, relay, window, base = arrays[a]
        start = (x + 4 - d) % 4
        if d:
            wait(relay.at[start], xr.at[a, d])

        def one(j, carry):
            to = (x + 1 + j) % 4
            if d:
                block = relay.at[start, :, :, pl.ds(pl.multiple_of(j * HD, HD), HD)]
            else:
                block = src.at[:, :, pl.ds(pl.multiple_of((3 * x + j) * HD, HD), HD)]
            place = window.at[pl.ds(base + start * 8 + head * 2, 2)]
            either(own_row & (to == y), block, place, ys.at[a], yr.at[a, start], device(x, to, z, y_lo))
            return carry

        lax.fori_loop(0, 3, one, 0)

    before = device(x, y, (z + 3 + core) % 4, 1 - core)
    after = device(x, y, (z + core) % 4, 1 - core)

    def forward(a, d):
        window = arrays[a][2]
        start = (x + 4 - d) % 4
        block = window.at[pl.ds(HALO + start * 8, 8)]
        wait(block, yr.at[a, start])

        @pl.when(start < 2)
        def _():
            place = window.at[pl.ds(HALO + ROW + start * 8, 8)]
            remote(block, place, fs.at[a], fr.at[a, 1], before).start()

        @pl.when(start >= 2)
        def _():
            place = window.at[pl.ds((start - 2) * 8, 8)]
            remote(block, place, fs.at[a], fr.at[a, 0], after).start()

    for d in range(1, 4):
        remote(lists_hbm, lists_r.at[x], ls, lxr.at[d], device((x + d) % 4, y, z, core)).start()
    own_lists = pltpu.make_async_copy(lists_hbm, lists_r.at[x], lc.at[0])
    own_lists.start()

    along_x(0)
    along_y(0, 0)
    along_x(1)
    along_y(1, 0)
    along_x(2)
    along_y(2, 0)

    own_lists.wait()
    for d in range(1, 4):
        wait(lists_r.at[x], lxr.at[d])

    @pl.when(head == 0)
    def _():
        for j in range(3):
            to = (x + 1 + j) % 4
            either(own_row & (to == y), lists_r, lists_v, ls, lyr, device(x, to, z, y_lo))

    for d in range(1, 4):
        along_y(0, d)

    @pl.when(active)
    def _():
        forward(0, 0)
        for d in range(1, 4):
            forward(0, d)

    for d in range(1, 4):
        along_y(1, d)

    @pl.when(active)
    def _():
        for d in range(4):
            forward(1, d)

    for d in range(1, 4):
        along_y(2, d)

    def out_x(d):
        to = (x + 4 - d) % 4
        wait(relay_o.at[to], oyr.at[d])
        columns = pl.ds(pl.multiple_of(x * GROUP, GROUP), GROUP)
        remote(relay_o.at[to], out_hbm.at[:, :, columns], oxs, oxr, device(to, y, z, core)).start()

    @pl.when(active)
    def _():
        wait(lists_v, lyr)
        to_scalar = pltpu.make_async_copy(lists_v, lists_s, lc.at[1])
        to_scalar.start()
        for a in range(2):
            for side in range(2):
                wait(win_k.at[pl.ds(0, HALO)], fr.at[a, side])
        to_scalar.wait()

        def attend(start, peer):
            for t in range(2):
                row = start * 8 + peer * 2 + t
                spots = [lists_s[start, peer * 2 + t, e] for e in range(SEL)]
                keys = jnp.concatenate([win_k[w] for w in spots], axis=0)
                scores = lax.dot_general(
                    win_q[row], keys, (((1,), (1,)), ((), ())), preferred_element_type=jnp.float32
                )
                peak = jnp.max(scores, axis=1, keepdims=True)
                weights = jnp.exp2((scores - peak) * EXP2)
                total = jnp.sum(weights, axis=1, keepdims=True)
                values = jnp.concatenate([win_v[w] for w in spots], axis=0)
                mixed = jnp.dot(weights.astype(jnp.bfloat16), values, preferred_element_type=jnp.float32)
                win_o[row] = (mixed / total).astype(jnp.bfloat16)

        for d in range(4):
            start = (x + 4 - d) % 4
            wait(win_q.at[pl.ds(start * 8, 8)], yr.at[2, start])

            def slot(peer, carry):
                attend(start, peer)
                block = win_o.at[pl.ds(start * 8 + peer * 2, 2)]
                to = {"head": peer, "blk": z * 8 + core * 4 + x}
                local = own_row & (peer == head)
                if d:
                    place = relay_o.at[start, :, :, pl.ds(pl.multiple_of(mine * HD, HD), HD)]
                    either(local, block, place, oys, oyr.at[d], to)
                else:
                    place = out_hbm.at[:, :, pl.ds(pl.multiple_of((3 * x + mine) * HD, HD), HD)]
                    either(local, block, place, oys, oxr, to)
                return carry

            lax.fori_loop(0, 4, slot, 0)
            if d >= 2:
                out_x(d - 1)
        out_x(3)

    @pl.when(jnp.logical_not(active))
    def _():
        for d in range(1, 4):
            out_x(d)

    wait(out_hbm, oxr)
    wait(relay_o.at[pl.ds(0, 3)], oxs)
    for d in range(3):
        wait(lists_r.at[x], ls)
    for a in range(3):
        wait(relay_k.at[pl.ds(0, 3)], xs.at[a])
    itself = own_row & active

    @pl.when(itself)
    def _():
        for a in range(3):
            wait(win_q.at[pl.ds(0, 16)], ys.at[a])
        wait(win_q.at[pl.ds(0, 24)], oys)

    @pl.when(jnp.logical_not(itself))
    def _():
        for a in range(3):
            wait(win_q.at[pl.ds(0, 24)], ys.at[a])

    @pl.when(active & jnp.logical_not(own_row))
    def _():
        wait(win_q, oys)

    @pl.when(active)
    def _():
        for a in range(2):
            wait(win_q, fs.at[a])

    @pl.when(head == 0)
    def _():
        for j in range(2):
            wait(lists_v, ls)

        @pl.when(jnp.logical_not(itself))
        def _():
            wait(lists_v, ls)


def local(queries, key_rows, value_rows, tile_lists):
    bf16, dma = jnp.bfloat16, pltpu.SemaphoreType.DMA
    relay = pltpu.VMEM((4, 2, TILE, GROUP), bf16)
    spots = (tile_lists + (256 + HALO - ROW * (lax.axis_index("blk") // 4))) % 256
    tiles = (2, TILE, queries.shape[1])
    result = pl.pallas_call(
        kernel,
        out_shape=jax.ShapeDtypeStruct(tiles, bf16),
        in_specs=[pl.BlockSpec(memory_space=pl.ANY)] * 4,
        out_specs=pl.BlockSpec(memory_space=pl.ANY),
        scratch_shapes=[
            relay, relay, relay, relay,
            pltpu.VMEM((2 * ROW, TILE, HD), bf16), pltpu.VMEM((2 * ROW, TILE, HD), bf16),
            pltpu.VMEM((ROW, TILE, HD), bf16), pltpu.VMEM((ROW, TILE, HD), bf16),
            pltpu.VMEM((4, 8, SEL), jnp.int32), pltpu.VMEM((4, 8, SEL), jnp.int32), pltpu.SMEM((4, 8, SEL), jnp.int32),
            dma((3,)), dma((3, 4)), dma((3,)), dma((3, 4)), dma((2,)), dma((2, 2)),
            dma, dma((4,)), dma, dma((2,)), dma, dma((4,)), dma, dma,
        ],
        compiler_params=pltpu.CompilerParams(collective_id=0, has_side_effects=True, vmem_limit_bytes=56 * 2**20),
        cost_estimate=pl.CostEstimate(flops=4 * 10**9, bytes_accessed=8 * 10**6, transcendentals=8 * 10**6),
    )(queries.reshape(tiles), key_rows.reshape(tiles), value_rows.reshape(tiles), spots)
    return result.reshape(queries.shape)


def solution(mesh):
    tokens = P(("blk", "head"), None)
    return jax.shard_map(
        local, mesh=mesh, in_specs=(tokens, tokens, tokens, P("blk", None)), out_specs=tokens, check_vma=False
    )
```

profile of v0, /device:TPU:11, one launch (start us, length us, event | category | flops | bytes accessed | tf_op | source)
XLA Modules:
  0.0 74.5 jit_solution(4567597470120150427)
XLA Ops:
  0.0 0.0 copy-start
  0.0 0.7 copy-done
  0.7 0.6 add_select_fusion.lists_hbm
  1.3 71.2 %shard_map.46 = bf16[2,128,1536]{2,1,0:T(8,128)(2,1)} custom-call(bf16[2,128,1536]{2,1,0:T(8,128)(2,1)} %bitcast.5, bf16[2,128,1536]{2,1,0:T(8,128)(2,1)} %bitcast.6, bf16[2,128,1536]{2,1,0:T(8,128)(2,1)} %bitcast.7, s32[8,16]{1,0:T(8,128)} %add_select_fusion.lists_hbm), custom_call_target="tpu_custom_call" | custom-call | flops 4000000000 | bytes 8000000 | tf_op jit(solution)/shard_map/pallas_call | solution.py:249
  72.5 2.1 %copy.6 = bf16[256,1536]{1,0:T(8,128)(2,1)} copy(bf16[256,1536]{1,0:T(8,128)(2,1)} %bitcast.4) | data formatting | bytes 1572864
Async XLA Ops:
  0.0 0.7 copy-start
where the time goes:
time: 74.7 us; the launch traced here: 74.5 us
  Pallas kernels  71.2 us (95%)
  local copies, waits for them, and re-layouts  2.75 us (4%)
    pallas_call x1, Pallas kernels, local(): pl.pallas_call(kernel, out_shape=jax.ShapeDtypeStruct(tiles, bf16), in_sp...  71.2 us
    unnamed x3, local copies, waits for them, and re-layouts  2.75 us

commit v1 on v0

--- a/solution.py
+++ b/solution.py
@@ -49,13 +49,13 @@
 
     barrier = pltpu.get_barrier_semaphore()
     for d in range(1, 4):
-        pl.semaphore_signal(barrier, inc=1, device_id=device((x + d) % 4, y, z, core), device_id_type=MESH)
         for c in range(2):
+            pl.semaphore_signal(barrier, inc=1, device_id=device((x + d) % 4, y, z, c), device_id_type=MESH)
             pl.semaphore_signal(barrier, inc=1, device_id=device(x, (y + d) % 4, z, c), device_id_type=MESH)
     pl.semaphore_signal(barrier, inc=1, device_id=device(x, y, z, 1 - core), device_id_type=MESH)
     across = device(x, y, (z + 2 * core + 3) % 4, 1 - core)
     pl.semaphore_signal(barrier, inc=1, device_id=across, device_id_type=MESH)
-    pl.semaphore_wait(barrier, 11)
+    pl.semaphore_wait(barrier, 14)
 
     arrays = ((k_hbm, relay_k, win_k, HALO), (v_hbm, relay_v, win_v, HALO), (q_hbm, relay_q, win_q, 0))
 
@@ -84,6 +84,37 @@
 
         lax.fori_loop(0, 3, one, 0)
 
+    def values_along_y():
+        for d in (2, 1, 3):
+            to = (y + d) % 4
+
+            def one(k, carry):
+                column = (to + 1 + k) % 4
+                block = v_hbm.at[:, :, pl.ds(pl.multiple_of((3 * column + 2 - k) * HD, HD), HD)]
+                remote(block, relay_v.at[y, k], xs.at[1], xr.at[1, d], device(x, to, z, core)).start()
+                return carry
+
+            lax.fori_loop(0, 3, one, 0)
+
+    def values_along_x(d):
+        source = (y + 4 - d) % 4
+        if d:
+            wait(relay_v.at[source, pl.ds(0, 3)], xr.at[1, d])
+
+        def one(k, carry):
+            to = (y + 1 + k) % 4
+            if d:
+                block = relay_v.at[source, k]
+            else:
+                block = v_hbm.at[:, :, pl.ds(pl.multiple_of((3 * to + 2 - k) * HD, HD), HD)]
+            peer = (source // 2) * 2 + core
+            place = win_v.at[pl.ds(HALO + x * 8 + peer * 2, 2)]
+            local = (to == x) & (source % 2 == core)
+            either(local, block, place, ys.at[1], yr.at[1, x], device(to, y, z, source % 2))
+            return carry
+
+        lax.fori_loop(0, 3, one, 0)
+
     before = device(x, y, (z + 3 + core) % 4, 1 - core)
     after = device(x, y, (z + core) % 4, 1 - core)
 
@@ -109,9 +140,12 @@
     own_lists.start()
 
     along_x(0)
+    values_along_y()
     along_y(0, 0)
-    along_x(1)
-    along_y(1, 0)
+    values_along_x(0)
+    for d in (1, 3, 2):
+        along_y(0, d)
+        values_along_x(d)
     along_x(2)
     along_y(2, 0)
 
@@ -125,24 +159,13 @@
             to = (x + 1 + j) % 4
             either(own_row & (to == y), lists_r, lists_v, ls, lyr, device(x, to, z, y_lo))
 
-    for d in range(1, 4):
-        along_y(0, d)
-
     @pl.when(active)
     def _():
-        forward(0, 0)
-        for d in range(1, 4):
-            forward(0, d)
-
-    for d in range(1, 4):
-        along_y(1, d)
-
-    @pl.when(active)
-    def _():
-        for d in range(4):
-            forward(1, d)
-
-    for d in range(1, 4):
+        for a in range(2):
+            for d in range(4):
+                forward(a, d)
+
+    for d in (1, 3, 2):
         along_y(2, d)
 
     def out_x(d):
@@ -161,42 +184,58 @@
                 wait(win_k.at[pl.ds(0, HALO)], fr.at[a, side])
         to_scalar.wait()
 
-        def attend(start, peer):
-            for t in range(2):
-                row = start * 8 + peer * 2 + t
-                spots = [lists_s[start, peer * 2 + t, e] for e in range(SEL)]
-                keys = jnp.concatenate([win_k[w] for w in spots], axis=0)
-                scores = lax.dot_general(
-                    win_q[row], keys, (((1,), (1,)), ((), ())), preferred_element_type=jnp.float32
-                )
+        def attend(start):
+            spots = [[lists_s[start, t, e] for e in range(SEL)] for t in range(8)]
+
+            def scores_of(t):
+                keys = jnp.concatenate([win_k[w] for w in spots[t]], axis=0)
+                query = win_q[start * 8 + t]
+                return lax.dot_general(query, keys, (((1,), (1,)), ((), ())), preferred_element_type=jnp.float32)
+
+            later = scores_of(0)
+            for t in range(8):
+                scores = later
+                if t < 7:
+                    later = scores_of(t + 1)
                 peak = jnp.max(scores, axis=1, keepdims=True)
                 weights = jnp.exp2((scores - peak) * EXP2)
                 total = jnp.sum(weights, axis=1, keepdims=True)
-                values = jnp.concatenate([win_v[w] for w in spots], axis=0)
+                values = jnp.concatenate([win_v[w] for w in spots[t]], axis=0)
                 mixed = jnp.dot(weights.astype(jnp.bfloat16), values, preferred_element_type=jnp.float32)
-                win_o[row] = (mixed / total).astype(jnp.bfloat16)
-
-        for d in range(4):
+                win_o[start * 8 + t] = (mixed / total).astype(jnp.bfloat16)
+
+        def quarter(i, carry):
+            d = (i + 1) % 4
             start = (x + 4 - d) % 4
             wait(win_q.at[pl.ds(start * 8, 8)], yr.at[2, start])
-
-            def slot(peer, carry):
-                attend(start, peer)
+            attend(start)
+
+            def send(peer, carry):
                 block = win_o.at[pl.ds(start * 8 + peer * 2, 2)]
                 to = {"head": peer, "blk": z * 8 + core * 4 + x}
                 local = own_row & (peer == head)
-                if d:
+
+                @pl.when(i < 3)
+                def _():
                     place = relay_o.at[start, :, :, pl.ds(pl.multiple_of(mine * HD, HD), HD)]
                     either(local, block, place, oys, oyr.at[d], to)
-                else:
+
+                @pl.when(i == 3)
+                def _():
                     place = out_hbm.at[:, :, pl.ds(pl.multiple_of((3 * x + mine) * HD, HD), HD)]
                     either(local, block, place, oys, oxr, to)
+
                 return carry
 
-            lax.fori_loop(0, 4, slot, 0)
-            if d >= 2:
-                out_x(d - 1)
-        out_x(3)
+            lax.fori_loop(0, 4, send, 0)
+
+            @pl.when(i >= 1)
+            def _():
+                out_x(i)
+
+            return carry
+
+        lax.fori_loop(0, 4, quarter, 0)
 
     @pl.when(jnp.logical_not(active))
     def _():
@@ -207,20 +246,29 @@
     wait(relay_o.at[pl.ds(0, 3)], oxs)
     for d in range(3):
         wait(lists_r.at[x], ls)
-    for a in range(3):
+    for a in (0, 2):
         wait(relay_k.at[pl.ds(0, 3)], xs.at[a])
+    wait(relay_v.at[pl.ds(0, 3), pl.ds(0, 3)], xs.at[1])
     itself = own_row & active
 
     @pl.when(itself)
     def _():
-        for a in range(3):
+        for a in (0, 2):
             wait(win_q.at[pl.ds(0, 16)], ys.at[a])
         wait(win_q.at[pl.ds(0, 24)], oys)
 
     @pl.when(jnp.logical_not(itself))
     def _():
-        for a in range(3):
+        for a in (0, 2):
             wait(win_q.at[pl.ds(0, 24)], ys.at[a])
+
+    @pl.when(active)
+    def _():
+        wait(win_q.at[pl.ds(0, 20)], ys.at[1])
+
+    @pl.when(jnp.logical_not(active))
+    def _():
+        wait(win_q.at[pl.ds(0, 24)], ys.at[1])
 
     @pl.when(active & jnp.logical_not(own_row))
     def _():
@@ -252,7 +300,7 @@
         in_specs=[pl.BlockSpec(memory_space=pl.ANY)] * 4,
         out_specs=pl.BlockSpec(memory_space=pl.ANY),
         scratch_shapes=[
-            relay, relay, relay, relay,
+            relay, pltpu.VMEM((4, 3, 2, TILE, HD), bf16), relay, relay,
             pltpu.VMEM((2 * ROW, TILE, HD), bf16), pltpu.VMEM((2 * ROW, TILE, HD), bf16),
             pltpu.VMEM((ROW, TILE, HD), bf16), pltpu.VMEM((ROW, TILE, HD), bf16),
             pltpu.VMEM((4, 8, SEL), jnp.int32), pltpu.VMEM((4, 8, SEL), jnp.int32), pltpu.SMEM((4, 8, SEL), jnp.int32),

time: 74.7 us -> 68.2 us (0.913)
  the two profiles are of different devices: /device:TPU:11 before, /device:TPU:1 now
where the time goes in v1:
time: 68.2 us; the launch traced here: 67.1 us
  Pallas kernels  63.7 us (93%)
  local copies, waits for them, and re-layouts  2.75 us (4%)
    pallas_call x1, Pallas kernels, local(): pl.pallas_call(kernel, out_shape=jax.ShapeDtypeStruct(tiles, bf16), in_sp...  63.7 us
    unnamed x3, local copies, waits for them, and re-layouts  2.75 us

profile of v1, /device:TPU:1, one launch (start us, length us, event | category | flops | bytes accessed | tf_op | source)
XLA Modules:
  0.0 67.1 jit_solution(827454528335008181)
XLA Ops:
  0.0 0.0 copy-start
  0.0 0.7 %copy-done = s32[8,16]{1,0:T(8,128)S(1)} copy-done((s32[8,16]{1,0:T(8,128)S(1)}, s32[8,16]{1,0:T(8,128)}, u32[]{:S(2)}) %copy-start) | copy-done | bytes 536
  0.7 0.6 add_select_fusion.lists_hbm
  1.3 63.7 %shard_map.46 = bf16[2,128,1536]{2,1,0:T(8,128)(2,1)} custom-call(bf16[2,128,1536]{2,1,0:T(8,128)(2,1)} %bitcast.5, bf16[2,128,1536]{2,1,0:T(8,128)(2,1)} %bitcast.6, bf16[2,128,1536]{2,1,0:T(8,128)(2,1)} %bitcast.7, s32[8,16]{1,0:T(8,128)} %add_select_fusion.lists_hbm), custom_call_target="tpu_custom_call" | custom-call | flops 4000000000 | bytes 8000000 | tf_op jit(solution)/shard_map/pallas_call | solution.py:297
  65.0 2.1 %copy.6 = bf16[256,1536]{1,0:T(8,128)(2,1)} copy(bf16[256,1536]{1,0:T(8,128)(2,1)} %bitcast.4) | data formatting | bytes 1572864
Async XLA Ops:
  0.0 0.7 %copy-start = (s32[8,16]{1,0:T(8,128)S(1)}, s32[8,16]{1,0:T(8,128)}, u32[]{:S(2)}) copy-start(s32[8,16]{1,0:T(8,128)} %param.7) | copy-start | bytes 1540

commit v2 on v1

v2 whole, which is shorter than its diff:
```python
import functools

import jax
import jax.numpy as jnp
from jax import lax
from jax.experimental import pallas as pl
from jax.experimental.pallas import tpu as pltpu
from jax.sharding import PartitionSpec as P

MESH = pl.DeviceIdType.MESH
HD = 128
TILE = 128
SEL = 16
GROUP = 3 * HD
ROW = 32
EXP2 = HD ** -0.5 * 1.4426950408889634


def kernel(q_hbm, k_hbm, v_hbm, lists_hbm, out_hbm, relay_k, relay_v, relay_q, relay_p, relay_o, near_k, near_v, far_k, far_v, win_q,
           win_o, lists_r, lists_v, lists_w, lists_s, xs, xr, ys, yr, fs, fr, fl, ls, lxr, lyr, lc, oys, oyr, oxs, oxr):
    head, blk = lax.axis_index("head"), lax.axis_index("blk")
    x, y_lo, z = blk % 4, (blk // 4) % 2, blk // 8
    core = head % 2
    y = (head // 2) * 2 + y_lo
    mine = (y + 7 - x) % 4
    active = mine < 3
    own_row = core == y_lo

    def device(dx, dy, dz, dc):
        return {"head": (dy // 2) * 2 + dc, "blk": dz * 8 + (dy % 2) * 4 + dx}

    def remote(src, dst, send, recv, to):
        return pltpu.make_async_remote_copy(
            src_ref=src, dst_ref=dst, send_sem=send, recv_sem=recv, device_id=to, device_id_type=MESH
        )

    def wait(ref, sem):
        pltpu.make_async_copy(ref, ref, sem).wait()

    def either(local, src, dst, send, recv, to):
        @pl.when(local)
        def _():
            pltpu.make_async_copy(src, dst, recv).start()

        @pl.when(jnp.logical_not(local))
        def _():
            remote(src, dst, send, recv, to).start()

    barrier = pltpu.get_barrier_semaphore()
    for d in range(1, 4):
        for c in range(2):
            pl.semaphore_signal(barrier, inc=1, device_id=device((x + d) % 4, y, z, c), device_id_type=MESH)
            pl.semaphore_signal(barrier, inc=1, device_id=device(x, (y + d) % 4, z, c), device_id_type=MESH)
    pl.semaphore_signal(barrier, inc=1, device_id=device(x, y, z, 1 - core), device_id_type=MESH)
    across = device(x, y, (z + 2 * core + 3) % 4, 1 - core)
    pl.semaphore_signal(barrier, inc=1, device_id=across, device_id_type=MESH)
    pl.semaphore_wait(barrier, 14)

    arrays = (
        (k_hbm, relay_k, near_k, 0, 2),
        (v_hbm, relay_v, near_v, 0, 2),
        (q_hbm, relay_q, win_q, 0, 1),
        (q_hbm, relay_p, win_q, 1, 1),
    )

    def turn(i, row):
        return (2 * (1 - row) + 2 * (i // 2)) % 4 + (x + 1 + i) % 2

    def along_x(a):
        src, relay, _, tile, count = arrays[a]
        for d in (2, 1, 3):
            to = (x + d) % 4
            columns = pl.ds(pl.multiple_of(to * GROUP, GROUP), GROUP)
            block = src.at[pl.ds(tile, count), :, columns]
            remote(block, relay.at[x], xs.at[a], xr.at[a, d], device(to, y, z, core)).start()

    def then_along_y(a, start, first):
        src, relay, window, tile, count = arrays[a]
        base = tile if a >= 2 else 16 * y_lo
        if not first:
            wait(relay.at[start], xr.at[a, (x + 4 - start) % 4])

        def one(j, carry):
            to = (x + 1 + j) % 4
            if first:
                block = src.at[pl.ds(tile, count), :, pl.ds(pl.multiple_of((3 * x + j) * HD, HD), HD)]
            else:
                block = relay.at[start, :, :, pl.ds(pl.multiple_of(j * HD, HD), HD)]
            place = window.at[pl.ds(base + start * 8 + head * 2, count)]
            either(own_row & (to == y), block, place, ys.at[a], yr.at[min(a, 2), start], device(x, to, z, y_lo))
            return carry

        lax.fori_loop(0, 3, one, 0)

    def others_along_y(a, i):
        start = turn(i, y_lo)

        @pl.when(start != x)
        def _():
            then_along_y(a, start, False)

    def along_y(a):
        src, relay, _, tile, count = arrays[a]
        for d in (2, 1, 3):
            to = (y + d) % 4

            def one(k, carry):
                column = (to + 1 + k) % 4
                columns = pl.ds(pl.multiple_of((3 * column + 2 - k) * HD, HD), HD)
                block = src.at[pl.ds(tile, count), :, columns]
                remote(block, relay.at[y, k], xs.at[a], xr.at[a, d], device(x, to, z, core)).start()
                return carry

            lax.fori_loop(0, 3, one, 0)

    def then_along_x(a, d):
        src, relay, window, tile, count = arrays[a]
        source = (y + 4 - d) % 4
        base = tile if a >= 2 else 16 * (source % 2)
        if d:
            wait(relay.at[source, pl.ds(0, 3)], xr.at[a, d])

        def one(k, carry):
            to = (y + 1 + k) % 4
            if d:
                block = relay.at[source, k]
            else:
                block = src.at[pl.ds(tile, count), :, pl.ds(pl.multiple_of((3 * to + 2 - k) * HD, HD), HD)]
            peer = (source // 2) * 2 + core
            place = window.at[pl.ds(base + x * 8 + peer * 2, count)]
            local = (to == x) & (source % 2 == core)
            either(local, block, place, ys.at[a], yr.at[min(a, 2), x], device(to, y, z, source % 2))
            return carry

        lax.fori_loop(0, 3, one, 0)

    sibling = device(x, y, z, 1 - core)

    def forward(a, start):
        near, far = ((near_k, far_k), (near_v, far_v))[a]
        block = near.at[pl.ds(16 * core + start * 8, 8)]
        wait(block, yr.at[a, start])

        @pl.when(start // 2 == core)
        def _():
            place = far.at[pl.ds(32 * (1 - core) + (start % 2) * 8, 8)]
            remote(block, place, fs.at[a], fr.at[a, 1], across).start()

        @pl.when(start // 2 != core)
        def _():
            place = near.at[pl.ds(32 * core + (start % 2) * 8, 8)]
            remote(block, place, fs.at[a], fr.at[a, 0], sibling).start()

        pltpu.make_async_copy(block, far.at[pl.ds(16 * (1 - core) + start * 8, 8)], fl.at[a]).start()

    for d in range(1, 4):
        remote(lists_hbm, lists_r.at[x], ls, lxr.at[d], device((x + d) % 4, y, z, core)).start()
    own_lists = pltpu.make_async_copy(lists_hbm, lists_r.at[x], lc.at[0])
    own_lists.start()

    along_x(0)
    along_y(1)
    then_along_y(0, x, True)
    then_along_x(1, 0)
    for i, d in ((2, 2), (3, 1), (0, 3), (1, None)):
        others_along_y(0, i)
        if d:
            then_along_x(1, d)
    along_x(2)
    along_y(3)
    then_along_y(2, x, True)
    then_along_x(3, 0)

    own_lists.wait()
    for d in range(1, 4):
        wait(lists_r.at[x], lxr.at[d])

    @pl.when(head == 0)
    def _():
        for j in range(3):
            to = (x + 1 + j) % 4
            either(own_row & (to == y), lists_r, lists_v, ls, lyr, device(x, to, z, y_lo))

    @pl.when(active)
    def _():
        for i in (2, 3, 0, 1):
            for a in range(2):
                forward(a, turn(i, core))

    for i, d in ((0, 2), (1, 1), (2, 3), (3, None)):
        others_along_y(2, i)
        if d:
            then_along_x(3, d)

    def out_x(i):
        to = turn(i, y_lo)

        @pl.when(to != x)
        def _():
            wait(relay_o.at[to], oyr.at[(x + 4 - to) % 4])
            columns = pl.ds(pl.multiple_of(x * GROUP, GROUP), GROUP)
            remote(relay_o.at[to], out_hbm.at[:, :, columns], oxs, oxr, device(to, y, z, core)).start()

    @pl.when(active)
    def _():
        wait(lists_v, lyr)
        for i in range(4):
            place = (lists_v[i] + (272 - ROW * (2 * z + core) - 16 * (i // 2))) & 255
            lists_w[i] = jnp.minimum(place, ROW + 15)
        to_scalar = pltpu.make_async_copy(lists_w, lists_s, lc.at[1])
        to_scalar.start()
        for a in range(2):
            wait(near_k.at[pl.ds(0, 16)], fr.at[a, 0])
        to_scalar.wait()

        def attend(start, keys_ref, values_ref):
            spots = [[lists_s[start, t, e] for e in range(SEL)] for t in range(8)]

            def scores_of(t):
                keys = jnp.concatenate([keys_ref[w] for w in spots[t]], axis=0)
                query = win_q[start * 8 + t]
                return lax.dot_general(query, keys, (((1,), (1,)), ((), ())), preferred_element_type=jnp.float32)

            later = scores_of(0)
            for t in range(8):
                scores = later
                if t < 7:
                    later = scores_of(t + 1)
                peak = jnp.max(scores, axis=1, keepdims=True)
                weights = jnp.exp2((scores - peak) * EXP2)
                total = jnp.sum(weights, axis=1, keepdims=True)
                values = jnp.concatenate([values_ref[w] for w in spots[t]], axis=0)
                mixed = jnp.dot(weights.astype(jnp.bfloat16), values, preferred_element_type=jnp.float32)
                win_o[start * 8 + t] = (mixed / total).astype(jnp.bfloat16)

        def quarter(i, keys_ref, values_ref):
            start = turn(i, core)
            wait(win_q.at[pl.ds(start * 8, 8)], yr.at[2, start])
            attend(start, keys_ref, values_ref)

            def send(peer, carry):
                block = win_o.at[pl.ds(start * 8 + peer * 2, 2)]
                to = {"head": peer, "blk": z * 8 + core * 4 + x}
                local = own_row & (peer == head)

                @pl.when(start != x)
                def _():
                    place = relay_o.at[start, :, :, pl.ds(pl.multiple_of(mine * HD, HD), HD)]
                    either(local, block, place, oys, oyr.at[(x + 4 - start) % 4], to)

                @pl.when(start == x)
                def _():
                    place = out_hbm.at[:, :, pl.ds(pl.multiple_of((3 * x + mine) * HD, HD), HD)]
                    either(local, block, place, oys, oxr, to)

                return carry

            lax.fori_loop(0, 4, send, 0)

        def first_half(i, carry):
            quarter(i, near_k, near_v)

            @pl.when(i == 1)
            def _():
                out_x(0)

            return carry

        def second_half(i, carry):
            quarter(i, far_k, far_v)
            out_x(i - 1)
            return carry

        lax.fori_loop(0, 2, first_half, 0)
        for a in range(2):
            wait(far_k.at[pl.ds(0, 16)], fr.at[a, 1])
            wait(far_k.at[pl.ds(0, 32)], fl.at[a])
        lax.fori_loop(2, 4, second_half, 0)
        out_x(3)

    @pl.when(jnp.logical_not(active))
    def _():
        for i in range(4):
            out_x(i)

    wait(out_hbm, oxr)
    wait(relay_o.at[pl.ds(0, 3)], oxs)
    for d in range(3):
        wait(lists_r.at[x], ls)
    wait(relay_k.at[pl.ds(0, 3)], xs.at[0])
    wait(relay_v.at[pl.ds(0, 3), pl.ds(0, 3)], xs.at[1])
    wait(relay_q.at[pl.ds(0, 3)], xs.at[2])
    wait(relay_p.at[pl.ds(0, 3), pl.ds(0, 3)], xs.at[3])
    itself = own_row & active

    @pl.when(itself)
    def _():
        wait(win_q.at[pl.ds(0, 16)], ys.at[0])
        wait(win_q.at[pl.ds(0, 8)], ys.at[2])
        wait(win_q.at[pl.ds(0, 24)], oys)

    @pl.when(jnp.logical_not(itself))
    def _():
        wait(win_q.at[pl.ds(0, 24)], ys.at[0])
        wait(win_q.at[pl.ds(0, 12)], ys.at[2])

    @pl.when(active)
    def _():
        wait(win_q.at[pl.ds(0, 20)], ys.at[1])
        wait(win_q.at[pl.ds(0, 10)], ys.at[3])

    @pl.when(jnp.logical_not(active))
    def _():
        wait(win_q.at[pl.ds(0, 24)], ys.at[1])
        wait(win_q.at[pl.ds(0, 12)], ys.at[3])

    @pl.when(active & jnp.logical_not(own_row))
    def _():
        wait(win_q, oys)

    @pl.when(active)
    def _():
        for a in range(2):
            wait(win_q, fs.at[a])

    @pl.when(head == 0)
    def _():
        for j in range(2):
            wait(lists_v, ls)

        @pl.when(jnp.logical_not(itself))
        def _():
            wait(lists_v, ls)


def local(queries, key_rows, value_rows, tile_lists):
    bf16, dma = jnp.bfloat16, pltpu.SemaphoreType.DMA
    relay = pltpu.VMEM((4, 2, TILE, GROUP), bf16)
    window = pltpu.VMEM((ROW + 16, TILE, HD), bf16)
    lists = pltpu.VMEM((4, 8, SEL), jnp.int32)
    tiles = (2, TILE, queries.shape[1])
    result = pl.pallas_call(
        kernel,
        out_shape=jax.ShapeDtypeStruct(tiles, bf16),
        in_specs=[pl.BlockSpec(memory_space=pl.ANY)] * 4,
        out_specs=pl.BlockSpec(memory_space=pl.ANY),
        scratch_shapes=[
            relay, pltpu.VMEM((4, 3, 2, TILE, HD), bf16),
            pltpu.VMEM((4, 1, TILE, GROUP), bf16), pltpu.VMEM((4, 3, 1, TILE, HD), bf16), relay,
            window, window, window, window,
            pltpu.VMEM((ROW, TILE, HD), bf16), pltpu.VMEM((ROW, TILE, HD), bf16),
            lists, lists, lists, pltpu.SMEM((4, 8, SEL), jnp.int32),
            dma((4,)), dma((4, 4)), dma((4,)), dma((3, 4)), dma((2,)), dma((2, 2)), dma((2,)),
            dma, dma((4,)), dma, dma((2,)), dma, dma((4,)), dma, dma,
        ],
        compiler_params=pltpu.CompilerParams(collective_id=0, has_side_effects=True, vmem_limit_bytes=56 * 2**20),
        cost_estimate=pl.CostEstimate(flops=4 * 10**9, bytes_accessed=8 * 10**6, transcendentals=8 * 10**6),
    )(queries.reshape(tiles), key_rows.reshape(tiles), value_rows.reshape(tiles), tile_lists)
    return result.reshape(queries.shape)


def solution(mesh):
    tokens = P(("blk", "head"), None)
    return jax.shard_map(
        local, mesh=mesh, in_specs=(tokens, tokens, tokens, P("blk", None)), out_specs=tokens, check_vma=False
    )
```

time: 68.2 us -> 65.8 us (0.965); the launches traced: 67.1 us -> 65.7 us
  local copies, waits for them, and re-layouts: 2.75 us -> 2.06 us
    unnamed x3 -> x1, local copies, waits for them, and re-layouts: 2.75 us -> 2.06 us
where the time goes in v2:
time: 65.8 us; the launch traced here: 65.7 us
  Pallas kernels  63.6 us (97%)
  local copies, waits for them, and re-layouts  2.06 us (3%)
    pallas_call x1, Pallas kernels, local(): pl.pallas_call(kernel, out_shape=jax.ShapeDtypeStruct(tiles, bf16), in_sp...  63.6 us
    unnamed x1, local copies, waits for them, and re-layouts  2.06 us

profile of v2, /device:TPU:1, one launch (start us, length us, event | category | flops | bytes accessed | tf_op | source)
XLA Modules:
  0.0 65.7 jit_solution(4483233145968184179)
XLA Ops:
  0.0 63.6 %shard_map.46 = bf16[2,128,1536]{2,1,0:T(8,128)(2,1)} custom-call(bf16[2,128,1536]{2,1,0:T(8,128)(2,1)} %bitcast.5, bf16[2,128,1536]{2,1,0:T(8,128)(2,1)} %bitcast.6, bf16[2,128,1536]{2,1,0:T(8,128)(2,1)} %bitcast.7, s32[8,16]{1,0:T(8,128)} %lists_hbm.1), custom_call_target="tpu_custom_call" | custom-call | flops 4000000000 | bytes 8000000 | tf_op jit(solution)/shard_map/pallas_call | solution.py:342
  63.6 2.1 %copy.6 = bf16[256,1536]{1,0:T(8,128)(2,1)} copy(bf16[256,1536]{1,0:T(8,128)(2,1)} %bitcast.4) | data formatting | bytes 1572864

commit v3 on v2

--- a/solution.py
+++ b/solution.py
@@ -16,8 +16,8 @@
 EXP2 = HD ** -0.5 * 1.4426950408889634
 
 
-def kernel(q_hbm, k_hbm, v_hbm, lists_hbm, out_hbm, relay_k, relay_v, relay_q, relay_p, relay_o, near_k, near_v, far_k, far_v, win_q,
-           win_o, lists_r, lists_v, lists_w, lists_s, xs, xr, ys, yr, fs, fr, fl, ls, lxr, lyr, lc, oys, oyr, oxs, oxr):
+def kernel(q_hbm, k_hbm, v_hbm, lists_hbm, out_hbm, relay_k, relay_v, relay_q, relay_p, relay_o, relay_r, near_k, near_v, far_k, far_v, win_q,
+           win_o, lists_r, lists_v, lists_w, lists_s, xs, xr, ys, yr, fs, fr, fl, ls, lxr, lyr, lc, oys, oyr, oxs, oxr, ofs, ofr, ors):
     head, blk = lax.axis_index("head"), lax.axis_index("blk")
     x, y_lo, z = blk % 4, (blk // 4) % 2, blk // 8
     core = head % 2
@@ -199,7 +199,26 @@
         def _():
             wait(relay_o.at[to], oyr.at[(x + 4 - to) % 4])
             columns = pl.ds(pl.multiple_of(x * GROUP, GROUP), GROUP)
-            remote(relay_o.at[to], out_hbm.at[:, :, columns], oxs, oxr, device(to, y, z, core)).start()
+            remote(relay_o.at[to], out_hbm.at[pl.ds(0, 1), :, columns], oxs, oxr, device(to, y, z, core)).start()
+
+    def out_y(i):
+        for k in range(1, 4):
+            start = (x + k) % 4
+            theirs = 2 * (1 - (x // 2 + core) % 2) + (x + start + 1) % 2
+
+            @pl.when((start != y) & (theirs == i))
+            def _():
+                wait(relay_r.at[start], ofr.at[start])
+                column = 3 * start + (y + 7 - start) % 4
+
+                def one(peer, carry):
+                    block = relay_r.at[start, pl.ds(peer, 1)]
+                    place = out_hbm.at[pl.ds(1, 1), :, pl.ds(pl.multiple_of(column * HD, HD), HD)]
+                    to = {"head": peer, "blk": z * 8 + core * 4 + x}
+                    either(own_row & (peer == head), block, place, ors, oxr, to)
+                    return carry
+
+                lax.fori_loop(0, 4, one, 0)
 
     @pl.when(active)
     def _():
@@ -231,25 +250,31 @@
                 total = jnp.sum(weights, axis=1, keepdims=True)
                 values = jnp.concatenate([values_ref[w] for w in spots[t]], axis=0)
                 mixed = jnp.dot(weights.astype(jnp.bfloat16), values, preferred_element_type=jnp.float32)
-                win_o[start * 8 + t] = (mixed / total).astype(jnp.bfloat16)
+                win_o[t % 2, start * 4 + t // 2] = (mixed / total).astype(jnp.bfloat16)
 
         def quarter(i, keys_ref, values_ref):
             start = turn(i, core)
             wait(win_q.at[pl.ds(start * 8, 8)], yr.at[2, start])
             attend(start, keys_ref, values_ref)
 
+            @pl.when(start != x)
+            def _():
+                block = win_o.at[1, pl.ds(start * 4, 4)]
+                remote(block, relay_r.at[x], ofs, ofr.at[x], device(start, y, z, core)).start()
+
             def send(peer, carry):
-                block = win_o.at[pl.ds(start * 8 + peer * 2, 2)]
                 to = {"head": peer, "blk": z * 8 + core * 4 + x}
                 local = own_row & (peer == head)
 
                 @pl.when(start != x)
                 def _():
+                    block = win_o.at[0, pl.ds(start * 4 + peer, 1)]
                     place = relay_o.at[start, :, :, pl.ds(pl.multiple_of(mine * HD, HD), HD)]
                     either(local, block, place, oys, oyr.at[(x + 4 - start) % 4], to)
 
                 @pl.when(start == x)
                 def _():
+                    block = win_o.at[:, start * 4 + peer]
                     place = out_hbm.at[:, :, pl.ds(pl.multiple_of((3 * x + mine) * HD, HD), HD)]
                     either(local, block, place, oys, oxr, to)
 
@@ -263,12 +288,14 @@
             @pl.when(i == 1)
             def _():
                 out_x(0)
+                out_y(0)
 
             return carry
 
         def second_half(i, carry):
             quarter(i, far_k, far_v)
             out_x(i - 1)
+            out_y(i - 1)
             return carry
 
         lax.fori_loop(0, 2, first_half, 0)
@@ -277,11 +304,13 @@
             wait(far_k.at[pl.ds(0, 32)], fl.at[a])
         lax.fori_loop(2, 4, second_half, 0)
         out_x(3)
+        out_y(3)
 
     @pl.when(jnp.logical_not(active))
     def _():
         for i in range(4):
             out_x(i)
+            out_y(i)
 
     wait(out_hbm, oxr)
     wait(relay_o.at[pl.ds(0, 3)], oxs)
@@ -297,7 +326,7 @@
     def _():
         wait(win_q.at[pl.ds(0, 16)], ys.at[0])
         wait(win_q.at[pl.ds(0, 8)], ys.at[2])
-        wait(win_q.at[pl.ds(0, 24)], oys)
+        wait(win_q.at[pl.ds(0, 15)], oys)
 
     @pl.when(jnp.logical_not(itself))
     def _():
@@ -314,12 +343,19 @@
         wait(win_q.at[pl.ds(0, 24)], ys.at[1])
         wait(win_q.at[pl.ds(0, 12)], ys.at[3])
 
+    for idle, own, count in ((0, 0, 8), (0, 1, 6), (1, 0, 12), (1, 1, 9)):
+
+        @pl.when((active if not idle else jnp.logical_not(active)) & (own_row if own else jnp.logical_not(own_row)))
+        def _():
+            wait(win_q.at[pl.ds(0, count)], ors)
+
     @pl.when(active & jnp.logical_not(own_row))
     def _():
-        wait(win_q, oys)
+        wait(win_q.at[pl.ds(0, 20)], oys)
 
     @pl.when(active)
     def _():
+        wait(win_q.at[pl.ds(0, 12)], ofs)
         for a in range(2):
             wait(win_q, fs.at[a])
 
@@ -346,12 +382,13 @@
         out_specs=pl.BlockSpec(memory_space=pl.ANY),
         scratch_shapes=[
             relay, pltpu.VMEM((4, 3, 2, TILE, HD), bf16),
-            pltpu.VMEM((4, 1, TILE, GROUP), bf16), pltpu.VMEM((4, 3, 1, TILE, HD), bf16), relay,
+            pltpu.VMEM((4, 1, TILE, GROUP), bf16), pltpu.VMEM((4, 3, 1, TILE, HD), bf16),
+            pltpu.VMEM((4, 1, TILE, GROUP), bf16), pltpu.VMEM((4, 4, TILE, HD), bf16),
             window, window, window, window,
-            pltpu.VMEM((ROW, TILE, HD), bf16), pltpu.VMEM((ROW, TILE, HD), bf16),
+            pltpu.VMEM((ROW, TILE, HD), bf16), pltpu.VMEM((2, ROW // 2, TILE, HD), bf16),
             lists, lists, lists, pltpu.SMEM((4, 8, SEL), jnp.int32),
             dma((4,)), dma((4, 4)), dma((4,)), dma((3, 4)), dma((2,)), dma((2, 2)), dma((2,)),
-            dma, dma((4,)), dma, dma((2,)), dma, dma((4,)), dma, dma,
+            dma, dma((4,)), dma, dma((2,)), dma, dma((4,)), dma, dma, dma, dma((4,)), dma,
         ],
         compiler_params=pltpu.CompilerParams(collective_id=0, has_side_effects=True, vmem_limit_bytes=56 * 2**20),
         cost_estimate=pl.CostEstimate(flops=4 * 10**9, bytes_accessed=8 * 10**6, transcendentals=8 * 10**6),

time: 65.8 us -> 63.1 us (0.959)
  Pallas kernels: 63.6 us -> 60.9 us
    pallas_call x1, Pallas kernels: 63.6 us -> 60.9 us  [local(): pl.pallas_call(kernel, out_shape=jax.ShapeDtypeStruct(tiles, bf16), in_sp...]
where the time goes in v3:
time: 63.1 us; the launch traced here: 63 us
  Pallas kernels  60.9 us (97%)
  local copies, waits for them, and re-layouts  2.06 us (3%)
    pallas_call x1, Pallas kernels, local(): pl.pallas_call(kernel, out_shape=jax.ShapeDtypeStruct(tiles, bf16), in_sp...  60.9 us
    unnamed x1, local copies, waits for them, and re-layouts  2.06 us

profile of v3, /device:TPU:1, one launch (start us, length us, event | category | flops | bytes accessed | tf_op | source)
XLA Modules:
  0.0 63.0 jit_solution(178587383161431818)
XLA Ops:
  0.0 60.9 %shard_map.46 = bf16[2,128,1536]{2,1,0:T(8,128)(2,1)} custom-call(bf16[2,128,1536]{2,1,0:T(8,128)(2,1)} %bitcast.5, bf16[2,128,1536]{2,1,0:T(8,128)(2,1)} %bitcast.6, bf16[2,128,1536]{2,1,0:T(8,128)(2,1)} %bitcast.7, s32[8,16]{1,0:T(8,128)} %lists_hbm.1), custom_call_target="tpu_custom_call" | custom-call | flops 4000000000 | bytes 8000000 | tf_op jit(solution)/shard_map/pallas_call | solution.py:378
  60.9 2.1 %copy.6 = bf16[256,1536]{1,0:T(8,128)(2,1)} copy(bf16[256,1536]{1,0:T(8,128)(2,1)} %bitcast.4) | data formatting | bytes 1572864

commit v4 on v3

--- a/solution.py
+++ b/solution.py
@@ -64,7 +64,10 @@
     )
 
     def turn(i, row):
-        return (2 * (1 - row) + 2 * (i // 2)) % 4 + (x + 1 + i) % 2
+        late = (x // 2 + row) % 2
+        return jnp.where(
+            i == 3, x, jnp.where(i == 2 * (1 - late), x + 1 - 2 * (x % 2), 2 * (1 - x // 2) + (x + 3 + i - late) % 2)
+        )
 
     def along_x(a):
         src, relay, _, tile, count = arrays[a]
@@ -162,10 +165,9 @@
     along_y(1)
     then_along_y(0, x, True)
     then_along_x(1, 0)
-    for i, d in ((2, 2), (3, 1), (0, 3), (1, None)):
+    for i, d in ((2, 2), (1, 1), (0, 3)):
         others_along_y(0, i)
-        if d:
-            then_along_x(1, d)
+        then_along_x(1, d)
     along_x(2)
     along_y(3)
     then_along_y(2, x, True)
@@ -183,14 +185,13 @@
 
     @pl.when(active)
     def _():
-        for i in (2, 3, 0, 1):
+        for i in (2, 1, 3, 0):
             for a in range(2):
                 forward(a, turn(i, core))
 
-    for i, d in ((0, 2), (1, 1), (2, 3), (3, None)):
+    for i, d in ((0, 2), (1, 1), (2, 3)):
         others_along_y(2, i)
-        if d:
-            then_along_x(3, d)
+        then_along_x(3, d)
 
     def out_x(i):
         to = turn(i, y_lo)
@@ -204,7 +205,8 @@
     def out_y(i):
         for k in range(1, 4):
             start = (x + k) % 4
-            theirs = 2 * (1 - (x // 2 + core) % 2) + (x + start + 1) % 2
+            late = (start // 2 + core) % 2
+            theirs = jnp.where(x // 2 == start // 2, 2 * (1 - late), (x + start + 1) % 2 + late)
 
             @pl.when((start != y) & (theirs == i))
             def _():
@@ -252,10 +254,23 @@
                 mixed = jnp.dot(weights.astype(jnp.bfloat16), values, preferred_element_type=jnp.float32)
                 win_o[t % 2, start * 4 + t // 2] = (mixed / total).astype(jnp.bfloat16)
 
-        def quarter(i, keys_ref, values_ref):
+        def quarter(i, carry):
             start = turn(i, core)
             wait(win_q.at[pl.ds(start * 8, 8)], yr.at[2, start])
-            attend(start, keys_ref, values_ref)
+
+            @pl.when(start // 2 != core)
+            def _():
+                attend(start, near_k, near_v)
+
+            @pl.when((start // 2 == core) & (i == 2 - (x // 2 + core) % 2))
+            def _():
+                for a in range(2):
+                    wait(far_k.at[pl.ds(0, 16)], fr.at[a, 1])
+                    wait(far_k.at[pl.ds(0, 32)], fl.at[a])
+
+            @pl.when(start // 2 == core)
+            def _():
+                attend(start, far_k, far_v)
 
             @pl.when(start != x)
             def _():
@@ -281,30 +296,12 @@
                 return carry
 
             lax.fori_loop(0, 4, send, 0)
-
-        def first_half(i, carry):
-            quarter(i, near_k, near_v)
-
-            @pl.when(i == 1)
-            def _():
-                out_x(0)
-                out_y(0)
-
             return carry
 
-        def second_half(i, carry):
-            quarter(i, far_k, far_v)
-            out_x(i - 1)
-            out_y(i - 1)
-            return carry
-
-        lax.fori_loop(0, 2, first_half, 0)
-        for a in range(2):
-            wait(far_k.at[pl.ds(0, 16)], fr.at[a, 1])
-            wait(far_k.at[pl.ds(0, 32)], fl.at[a])
-        lax.fori_loop(2, 4, second_half, 0)
-        out_x(3)
-        out_y(3)
+        lax.fori_loop(0, 4, quarter, 0)
+        for i in range(4):
+            out_x(i)
+            out_y(i)
 
     @pl.when(jnp.logical_not(active))
     def _():

time: 63.1 us -> 61.4 us (0.973)
  Pallas kernels: 60.9 us -> 59.2 us
    pallas_call x1, Pallas kernels: 60.9 us -> 59.2 us  [local(): pl.pallas_call(kernel, out_shape=jax.ShapeDtypeStruct(tiles, bf16), in_sp...]
where the time goes in v4:
time: 61.4 us; the launch traced here: 61.2 us
  Pallas kernels  59.2 us (96%)
  local copies, waits for them, and re-layouts  2.06 us (3%)
    pallas_call x1, Pallas kernels, local(): pl.pallas_call(kernel, out_shape=jax.ShapeDtypeStruct(tiles, bf16), in_sp...  59.2 us
    unnamed x1, local copies, waits for them, and re-layouts  2.06 us

profile of v4, /device:TPU:1, one launch (start us, length us, event | category | flops | bytes accessed | tf_op | source)
XLA Modules:
  0.0 61.2 jit_solution(5965080931075845439)
XLA Ops:
  0.0 59.2 %shard_map.46 = bf16[2,128,1536]{2,1,0:T(8,128)(2,1)} custom-call(bf16[2,128,1536]{2,1,0:T(8,128)(2,1)} %bitcast.5, bf16[2,128,1536]{2,1,0:T(8,128)(2,1)} %bitcast.6, bf16[2,128,1536]{2,1,0:T(8,128)(2,1)} %bitcast.7, s32[8,16]{1,0:T(8,128)} %lists_hbm.1), custom_call_target="tpu_custom_call" | custom-call | flops 4000000000 | bytes 8000000 | tf_op jit(solution)/shard_map/pallas_call | solution.py:375
  59.2 2.1 %copy.6 = bf16[256,1536]{1,0:T(8,128)(2,1)} copy(bf16[256,1536]{1,0:T(8,128)(2,1)} %bitcast.4) | data formatting | bytes 1572864

commit v5 on v4

--- a/solution.py
+++ b/solution.py
@@ -168,24 +168,31 @@
     for i, d in ((2, 2), (1, 1), (0, 3)):
         others_along_y(0, i)
         then_along_x(1, d)
+
+    own_lists.wait()
+    for d in range(1, 4):
+        wait(lists_r.at[x], lxr.at[d])
+
+    @pl.when(head == 0)
+    def _():
+        for j in range(3):
+            to = (x + 1 + j) % 4
+            either(own_row & (to == y), lists_r, lists_v, ls, lyr, device(x, to, z, y_lo))
+
+    @pl.when(active)
+    def _():
+        for i in (3, 2):
+            for a in range(2):
+                forward(a, turn(i, core))
+
     along_x(2)
     along_y(3)
     then_along_y(2, x, True)
     then_along_x(3, 0)
 
-    own_lists.wait()
-    for d in range(1, 4):
-        wait(lists_r.at[x], lxr.at[d])
-
-    @pl.when(head == 0)
-    def _():
-        for j in range(3):
-            to = (x + 1 + j) % 4
-            either(own_row & (to == y), lists_r, lists_v, ls, lyr, device(x, to, z, y_lo))
-
     @pl.when(active)
     def _():
-        for i in (2, 1, 3, 0):
+        for i in (1, 0):
             for a in range(2):
                 forward(a, turn(i, core))
 

time: 61.4 us -> 60.7 us (0.989)
  Pallas kernels: 59.2 us -> 58.5 us
    pallas_call x1, Pallas kernels: 59.2 us -> 58.5 us  [local(): pl.pallas_call(kernel, out_shape=jax.ShapeDtypeStruct(tiles, bf16), in_sp...]
where the time goes in v5:
time: 60.7 us; the launch traced here: 60.6 us
  Pallas kernels  58.5 us (96%)
  local copies, waits for them, and re-layouts  2.06 us (3%)
    pallas_call x1, Pallas kernels, local(): pl.pallas_call(kernel, out_shape=jax.ShapeDtypeStruct(tiles, bf16), in_sp...  58.5 us
    unnamed x1, local copies, waits for them, and re-layouts  2.06 us

profile of v5, /device:TPU:1, one launch (start us, length us, event | category | flops | bytes accessed | tf_op | source)
XLA Modules:
  0.0 60.6 jit_solution(278947908743366397)
XLA Ops:
  0.0 58.5 %shard_map.46 = bf16[2,128,1536]{2,1,0:T(8,128)(2,1)} custom-call(bf16[2,128,1536]{2,1,0:T(8,128)(2,1)} %bitcast.5, bf16[2,128,1536]{2,1,0:T(8,128)(2,1)} %bitcast.6, bf16[2,128,1536]{2,1,0:T(8,128)(2,1)} %bitcast.7, s32[8,16]{1,0:T(8,128)} %lists_hbm.1), custom_call_target="tpu_custom_call" | custom-call | flops 4000000000 | bytes 8000000 | tf_op jit(solution)/shard_map/pallas_call | solution.py:382
  58.5 2.1 %copy.6 = bf16[256,1536]{1,0:T(8,128)(2,1)} copy(bf16[256,1536]{1,0:T(8,128)(2,1)} %bitcast.4) | data formatting | bytes 1572864
